TPU v7x, 256 devices: a whole 4x4x8 slice. The times are simulated.
256 devices in a mesh: row: 4 (over x), col: 8 (over z_lo, core), depth: 8 (over z_hi, y).
Axes of the slice: x: 4, y: 4, z: 8 (z_hi: 2, z_lo: 4; z = z_hi * 4 + z_lo), core: 2. Of those that a mesh axis runs over, the one named last changes fastest.
Arguments:
- left_panel: float32 [8192, 2048], P(('row', 'col'), 'depth'), may hold values from -1 to 1
- upper_inverse: float32 [2048, 2048], P(None, 'depth'), as said below
- lower_inverse: float32 [2048, 2048], P('depth'), as said below
- top_panel: float32 [2048, 8192], P('depth', 'col'), may hold values from -1 to 1
- trailing: float32 [8192, 8192], P('row', ('col', 'depth')), may hold values from -6 to 6
Outputs:
- schur_block: float32 [8192, 8192], P('row', ('col', 'depth'))
Inputs may be any that keep to these rules, and one draw needn't show every extreme that they name: `upper_inverse`: zero below the diagonal. `lower_inverse`: zero above the diagonal.
All inputs are finite; a program needn't handle non-finite values.
Results may differ from a plain program's by a relative error of at most 0.00005.
Values sent between devices are 32-bit elements; how exact they have to be, the bound alone decides.
A program may use at most 128 MiB of HBM per device.

v0:
```python
import jax
import jax.numpy as jnp
from jax import lax
from jax.sharding import PartitionSpec as P


def local(left_panel, upper_inverse, lower_inverse, top_panel, trailing):
    highest = lax.Precision.HIGHEST
    factor = upper_inverse
    solved_part = jnp.dot(
        lax.all_gather(left_panel, "depth", axis=1, tiled=True),
        factor,
        precision=highest,
        preferred_element_type=jnp.float32,
    )
    solved_cols = lax.all_gather(solved_part, "col", axis=0, tiled=True)
    factor = lower_inverse
    projected = jnp.dot(
        factor,
        lax.all_gather(top_panel, "depth", axis=0, tiled=True),
        precision=highest,
        preferred_element_type=jnp.float32,
    )
    summed = lax.psum_scatter(
        lax.dot_general(
            projected,
            solved_cols,
            (((0,), (1,)), ((), ())),
            precision=highest,
            preferred_element_type=jnp.float32,
        ),
        "depth",
        scatter_dimension=0,
        tiled=True,
    )
    return trailing - summed.T


def solution(mesh):
    placed = (
        P(("row", "col"), "depth"),
        P(None, "depth"),
        P("depth", None),
        P("depth", "col"),
        P("row", ("col", "depth")),
    )
    return jax.shard_map(
        local, mesh=mesh, in_specs=placed, out_specs=P("row", ("col", "depth")), check_vma=False
    )
```

profile of v0, /device:TPU:64, one launch (start us, length us, event | category | flops | bytes accessed | tf_op | source)
XLA Modules:
  0.0 509.1 jit_solution(10727790279112978435)
XLA Ops:
  6.5 0.0 copy-start
  6.5 0.0 all-gather.6.cloned.1.call-start
  6.5 0.7 all-gather.6.cloned.1.call-update
  7.3 0.0 all-gather.4.cloned.1.call-start
  7.3 0.7 all-gather.4.cloned.1.call-update
  8.0 0.0 all-gather.8.cloned.1.call-start
  8.1 78.6 %all-gather.6.cloned.1.call-done = f32[256,2048]{1,0:T(8,128)} async-done(((f32[256,256]{1,0:T(8,128)}), f32[256,2048]{1,0:T(8,128)}) %all-gather.6.cloned.1.call-update) | async-done | bytes 2097168 | tf_op jit(solution)/shard_map/all_gather | solution.py:11
  86.6 4.8 fusion.1
  91.4 0.0 all-gather.8.cloned.1.call-update
  91.5 0.0 reduce-scatter.2.cloned.1.call-start
  91.5 166.3 %all-gather.4.cloned.1.call-done = f32[2048,1024]{1,0:T(8,128)} async-done(((f32[256,1024]{1,0:T(8,128)}), f32[2048,1024]{1,0:T(8,128)}) %all-gather.4.cloned.1.call-update) | async-done | bytes 8388624 | tf_op jit(solution)/shard_map/all_gather | solution.py:20
  257.8 0.0 copy-done
  257.8 9.8 %fusion = f32[256,1024]{1,0:T(8,128)S(1)} fusion(f32[256,2048]{1,0:T(8,128)S(1)} %copy-done, f32[2048,1024]{1,0:T(8,128)} %all-gather.4.cloned.1.call-done), kind=kOutput, calls=%fused_computation.1 | convolution fusion | flops 6442450944 | bytes 11534336 | tf_op jit(solution)/shard_map/dot_general | solution.py:18
  267.7 23.8 %all-gather.8.cloned.1.call-done = f32[2048,256]{1,0:T(8,128)} async-done(((f32[256,256]{1,0:T(8,128)}), f32[2048,256]{1,0:T(8,128)}) %all-gather.8.cloned.1.call-update) | async-done | bytes 2097168 | tf_op jit(solution)/shard_map/all_gather | solution.py:16
  291.5 16.7 %fusion.2 = f32[1024,2048]{1,0:T(8,128)} fusion(f32[256,1024]{1,0:T(8,128)S(1)} %fusion, f32[2048,256]{1,0:T(8,128)} %all-gather.8.cloned.1.call-done), kind=kOutput, calls=%fused_computation.3 | convolution fusion | flops 6442450944 | bytes 11534336 | tf_op jit(solution)/shard_map/dot_general | solution.py:25
  308.2 0.0 reduce-scatter.2.cloned.1.call-update
  308.2 1.6 copy.6
  309.8 187.9 %reduce-scatter.2.cloned.1.call-done = f32[128,2048]{1,0:T(8,128)} async-done(((f32[1024,2048]{1,0:T(8,128)}), f32[128,2048]{1,0:T(8,128)}) %reduce-scatter.2.cloned.1.call-update) | async-done | bytes 1048592 | tf_op jit(solution)/shard_map/reduce_scatter | solution.py:24
  497.8 2.3 bitcast_subtract_fusion
  500.1 2.5 copy.7
Async XLA Ops:
  6.5 251.3 %copy-start = (f32[256,2048]{1,0:T(8,128)S(1)}, f32[256,2048]{1,0:T(8,128)}, u32[]{:S(2)}) copy-start(f32[256,2048]{1,0:T(8,128)} %param.7) | copy-start | bytes 6291460
  6.5 80.1 %all-gather.6.cloned.1.call-start = ((), (), s32[]{:S(2)}) async-start(), calls=%async_computation.2 | async-start | bytes 2359296 | tf_op jit(solution)/shard_map/all_gather | solution.py:11
  7.3 250.6 %all-gather.4.cloned.1.call-start = ((), (), s32[]{:S(2)}) async-start(), calls=%async_computation.1 | async-start | bytes 9437184 | tf_op jit(solution)/shard_map/all_gather | solution.py:20
  8.0 283.5 %all-gather.8.cloned.1.call-start = ((), (), s32[]{:S(2)}) async-start(), calls=%async_computation.3 | async-start | bytes 2359296 | tf_op jit(solution)/shard_map/all_gather | solution.py:16
  91.5 406.3 %reduce-scatter.2.cloned.1.call-start = ((), (), s32[]{:S(2)}) async-start(), calls=%async_computation.4 | async-start | bytes 9437184 | tf_op jit(solution)/shard_map/reduce_scatter | solution.py:24
Sparse Core Ops, SparseCore 0:
  9.8 76.7 all-gather.5
  89.3 168.5 all-gather.3
  259.6 31.8 all-gather.7
  308.4 189.3 reduce-scatter.1
where the time goes:
time: 512 us; the launch traced here: 509 us
  waiting for transfers between devices  458 us (89%)
  matrix products  31.3 us (6%)
  between operations  13.1 us (3%)
    reduce_scatter x1, waiting for transfers between devices, local(): lax.psum_scatter(lax.dot_general(projected, solved_cols, (((0,), (1,)), (...  188 us
    all_gather x1, waiting for transfers between devices, local(): lax.all_gather(top_panel, 'depth', axis=0, tiled=True)  166 us
    all_gather x1, waiting for transfers between devices, local(): lax.all_gather(left_panel, 'depth', axis=1, tiled=True)  78.6 us
    all_gather x1, waiting for transfers between devices, local(): solved_cols = lax.all_gather(solved_part, 'col', axis=0, tiled=True)  23.8 us
    dot_general x1, matrix products, local(): lax.dot_general(projected, solved_cols, (((0,), (1,)), ((), ())), precisi...  16.7 us
  transfers between devices with their start and end apart: 4, of which 4 were waited for; matrix products, arithmetic and copies ran while one was open for 3% of the time, Pallas kernels for 0%

commit v1 on v0

v1 whole, which is shorter than its diff:
```python
import functools

import jax
import jax.numpy as jnp
from jax import lax
from jax.experimental import pallas as pl
from jax.experimental.pallas import tpu as pltpu
from jax.sharding import PartitionSpec as P

MESH = pl.DeviceIdType.MESH
F32 = jnp.float32
BF16 = jnp.bfloat16
B = 256


def split(v):
    high = v.astype(BF16)
    return high, (v - high.astype(F32)).astype(BF16)


def mm3(a, b):
    (ah, al), (bh, bl) = a, b
    dot = functools.partial(jnp.dot, preferred_element_type=F32)
    return dot(ah, bh) + (dot(ah, bl) + dot(al, bh))


def kernel(
    left, upper, lower, top, trailing, out,
    gbuf, ubuf, lbuf, sbuf, tloc, tbuf, th, tl, pbuf, rbuf,
    gsem, xsend, gsend, fsem, fsend, tsem, tsend, rsem, rsend, csem, csend, psem, psend,
):
    x = lax.axis_index("row")
    c = lax.axis_index("col")
    d = lax.axis_index("depth")
    k = lax.rem(c, 2)
    zl = c // 2
    y = lax.rem(d, 4)
    zh = d // 4
    z = zh * 4 + zl
    d2 = (1 - zh) * 4 + y

    def dev(x_, y_, z_, k_):
        return (x_, lax.rem(z_, 4) * 2 + k_, (z_ // 4) * 4 + y_)

    def rot4(v, by):
        return lax.rem(v + by, 4)

    def rot8(v, by):
        return lax.rem(v + by + 8, 8)

    def remote(src, dst, ss, rs, device):
        return pltpu.make_async_remote_copy(
            src_ref=src, dst_ref=dst, send_sem=ss, recv_sem=rs, device_id=device, device_id_type=MESH
        )

    def landed(ref, sem):
        pltpu.make_async_copy(ref, ref, sem).wait()

    zo = rot8(z, 4)
    z_up, z_down = rot8(z, 1), rot8(z, -1)

    peers = [dev(x, y, z, 1 - k), dev(x, y, zo, 0), dev(x, y, zo, 1), dev(x, y, z_up, k), dev(x, y, z_down, k)]
    peers += [dev(x, rot4(y, i), z, k) for i in (1, 2, 3)]
    peers += [dev(rot4(x, i), y, z, j) for i in (1, 2, 3) for j in (0, 1)]
    barrier = pltpu.get_barrier_semaphore()
    for peer in peers:
        pl.semaphore_signal(barrier, inc=1, device_id=peer, device_id_type=MESH)
    pl.semaphore_wait(barrier, len(peers))

    sends = []

    def start(cp, when=None):
        if when is None:
            cp.start()
        else:
            pl.when(when)(lambda: cp.start())
        sends.append((cp, when))

    is_self = jnp.logical_and(k == 0, zh == 0)
    start(
        remote(left, gbuf.at[d], xsend.at[0], gsem.at[d], dev(x, y, k * 4 + zl, 0)),
        jnp.logical_not(is_self),
    )
    pl.when(is_self)(lambda: pltpu.make_async_copy(left, gbuf.at[d], gsem.at[d]).start())

    mine = k == x // 2
    for h in (0, 1):
        block = top.at[:, pl.ds(pl.multiple_of(h * 512 + lax.rem(x, 2) * B, B), B)]
        own = jnp.logical_and(k == 1, zh == h)
        start(
            remote(block, gbuf.at[d], xsend.at[1 + h], gsem.at[d], dev(x, y, h * 4 + zl, 1)),
            jnp.logical_and(mine, jnp.logical_not(own)),
        )
        pl.when(jnp.logical_and(mine, own))(
            lambda: pltpu.make_async_copy(block, gbuf.at[d], gsem.at[d]).start()
        )

    edge = jnp.logical_or(zl == 0, zl == 3)
    z_cross = jnp.where(zl == 0, z_down, z_up)
    z_in = jnp.where(zl == 0, z_up, z_down)
    uq = upper.at[pl.ds(pl.multiple_of(x * 512, 512), 512), :]
    lq = lower.at[:, pl.ds(pl.multiple_of(x * 512, 512), 512)]
    is0, is1 = k == 0, k == 1
    for is_k, src, buf in ((is0, uq, ubuf), (is1, lq, lbuf)):
        start(
            remote(src, buf.at[x], fsend.at[0], fsem.at[x], dev(x, y, z_cross, k)),
            jnp.logical_and(edge, is_k),
        )

    def gather_y(slot, j):
        for i in (1, 2, 3):
            yy = rot4(y, i)
            start(
                remote(gbuf.at[slot], gbuf.at[slot], gsend.at[j, i - 1], gsem.at[slot], dev(x, yy, z, k)),
                jnp.logical_or(slot < 4, yy > y),
            )

    landed(gbuf.at[d], gsem.at[d])
    gather_y(d, 0)
    landed(ubuf.at[0], fsem.at[x])
    for is_k, buf in ((is0, ubuf), (is1, lbuf)):
        start(
            remote(buf.at[x], buf.at[x], fsend.at[1], fsem.at[x], dev(x, y, z_in, k)),
            jnp.logical_and(edge, is_k),
        )
        for i in (1, 2, 3):
            start(
                remote(buf.at[x], buf.at[x], fsend.at[1 + i], fsem.at[x], dev(rot4(x, i), y, z, k)),
                is_k,
            )
    landed(gbuf.at[d2], gsem.at[d2])
    gather_y(d2, 1)

    def wait_block(i):
        other_y = lax.rem(i, 4) != y

        @pl.when(jnp.logical_and(other_y, i <= 4 + y))
        def _():
            landed(gbuf.at[i], gsem.at[i])

        q = i // 2

        @pl.when(jnp.logical_and(lax.rem(i, 2) == 0, q != x))
        def _():
            landed(ubuf.at[q], fsem.at[q])

    @pl.when(k == 0)
    def _():
        sbuf[z] = jnp.zeros((2, B, B), F32)

        @pl.loop(0, 8)
        def _(i):
            wait_block(i)

            @pl.when(i <= d)
            def _():
                f = upper[pl.ds(pl.multiple_of(i * B, B), B), :]
                sbuf[z, zh] += mm3(split(gbuf[i]), split(f))

            @pl.when(i <= d2)
            def _():
                f = ubuf[i // 2, pl.ds(pl.multiple_of(lax.rem(i, 2) * B, B), B), :]
                sbuf[z, 1 - zh] += mm3(split(gbuf[i]), split(f))

        remote(sbuf.at[z], sbuf.at[z], csend.at[0], csem.at[0], dev(x, y, z, 1)).start()

    t_core = x // 2
    t_slot = lax.rem(x, 2)

    @pl.when(k == 1)
    def _():
        tloc[...] = jnp.zeros((2, B, B), F32)

        @pl.loop(0, 8)
        def _(i):
            wait_block(i)

            @pl.when(i <= d)
            def _():
                f = lower[:, pl.ds(pl.multiple_of(i * B, B), B)]
                tloc[zh] += mm3(split(f), split(gbuf[i]))

            @pl.when(i <= d2)
            def _():
                f = lbuf[i // 2, :, pl.ds(pl.multiple_of(lax.rem(i, 2) * B, B), B)]
                tloc[1 - zh] += mm3(split(f), split(gbuf[i]))

    for i in range(4):
        own = jnp.logical_and(t_core == 1, i == 0)
        start(
            remote(tloc, tbuf.at[t_slot], tsend.at[i], tsem.at[t_slot], dev(rot4(x, i), y, z, t_core)),
            jnp.logical_and(is1, jnp.logical_not(own)),
        )
    pl.when(jnp.logical_and(is1, t_core == 1))(
        lambda: pltpu.make_async_copy(tloc, tbuf.at[t_slot], tsem.at[t_slot]).start()
    )

    def piece(i):
        s = (i + 1) // 2
        return rot8(z, jnp.where(lax.rem(i, 2) == 1, -s, s))

    half = pl.ds(pl.multiple_of(k * 128, 128), 128)
    other_half = pl.ds(pl.multiple_of((1 - k) * 128, 128), 128)

    def ring(p, ss, i, z_):
        r = sbuf.at[p, :, half, :]
        return remote(r, r, ss, rsem.at[i], dev(x, y, z_, k))

    def to_sibling(p, i):
        r = sbuf.at[p, :, half, :]
        return remote(r, r, csend.at[i], csem.at[i], dev(x, y, z, 1 - k))

    def arrive(i):
        p = piece(i)
        landed(sbuf.at[p, :, half, :], rsem.at[i])
        odd = lax.rem(i, 2) == 1
        pl.when(jnp.logical_and(odd, i < 7))(lambda: ring(p, rsend.at[i], i + 2, z_up).start())
        pl.when(jnp.logical_and(jnp.logical_not(odd), i < 6))(lambda: ring(p, rsend.at[i], i + 2, z_down).start())
        to_sibling(p, i).start()

    def rows_of(p):
        return pl.ds(pl.multiple_of((2 * lax.rem(p, 4) + p // 4) * B, B), B)

    def partial_copy(i, j):
        rows = rows_of(piece(i))
        yy = rot4(y, j)
        return remote(pbuf.at[i, yy], rbuf.at[j - 1, rows], psend.at[j - 1, i], psem.at[j - 1, i], dev(x, yy, z, k))

    def process(i):
        p = piece(i)
        rows = rows_of(p)
        a = [split(sbuf[p, n]) for n in (0, 1)]
        for h in (0, 1):
            acc = mm3(a[0], (th[h, 0], tl[h, 0])) + mm3(a[1], (th[h, 1], tl[h, 1]))
            pbuf[i, 2 * h] = acc[:, :128]
            pbuf[i, 2 * h + 1] = acc[:, 128:]
        for j in (1, 2, 3):
            partial_copy(i, j).start()
        out[rows, :] = trailing[rows, :] - pbuf[i, y]

    @pl.when(k == 1)
    def _():
        landed(sbuf.at[z], csem.at[0])

    ring(z, rsend.at[0], 1, z_up).start()
    ring(z, rsend.at[8], 2, z_down).start()

    for h in (0, 1):
        landed(tbuf.at[h], tsem.at[h])
        for n in (0, 1):
            high, low = split(tbuf[h, n])
            th[h, n] = high
            tl[h, n] = low

    process(0)

    @pl.loop(1, 9)
    def _(i):
        pl.when(i < 8)(lambda: arrive(i))

        @pl.when(i > 1)
        def _():
            landed(sbuf.at[piece(i - 1), :, other_half, :], csem.at[i - 1])
            process(i - 1)

    @pl.loop(0, 8)
    def _(i):
        rows = rows_of(piece(i))
        for j in (1, 2, 3):
            landed(rbuf.at[j - 1, rows], psem.at[j - 1, i])
        out[rows, :] = out[rows, :] - ((rbuf[0, rows] + rbuf[1, rows]) + rbuf[2, rows])

    for cp, when in sends:
        if when is None:
            cp.wait_send()
        else:
            pl.when(when)(lambda: cp.wait_send())

    @pl.when(k == 0)
    def _():
        remote(sbuf.at[z], sbuf.at[z], csend.at[0], csem.at[0], dev(x, y, z, 1)).wait_send()

    ring(z, rsend.at[0], 1, z_up).wait_send()
    ring(z, rsend.at[8], 2, z_down).wait_send()

    @pl.loop(1, 8)
    def _(i):
        pl.when(i < 6)(lambda: ring(z, rsend.at[i], i + 2, z_up).wait_send())
        to_sibling(z, i).wait_send()

    @pl.loop(0, 8)
    def _(i):
        for j in (1, 2, 3):
            partial_copy(i, j).wait_send()


def local(left_panel, upper_inverse, lower_inverse, top_panel, trailing):
    vmem = pl.BlockSpec(memory_space=pltpu.VMEM)
    dma = pltpu.SemaphoreType.DMA
    return pl.pallas_call(
        kernel,
        out_shape=jax.ShapeDtypeStruct(trailing.shape, F32),
        in_specs=[vmem] * 5,
        out_specs=vmem,
        scratch_shapes=[
            pltpu.VMEM((8, B, B), F32),
            pltpu.VMEM((4, 512, B), F32),
            pltpu.VMEM((4, B, 512), F32),
            pltpu.VMEM((8, 2, B, B), F32),
            pltpu.VMEM((2, B, B), F32),
            pltpu.VMEM((2, 2, B, B), F32),
            pltpu.VMEM((2, 2, B, B), BF16),
            pltpu.VMEM((2, 2, B, B), BF16),
            pltpu.VMEM((8, 4, B, 128), F32),
            pltpu.VMEM((3, 2048, 128), F32),
            dma((8,)), dma((3,)), dma((2, 3)), dma((4,)), dma((5,)), dma((2,)), dma((4,)),
            dma((8,)), dma((9,)), dma((8,)), dma((8,)), dma((3, 8)), dma((3, 8)),
        ],
        compiler_params=pltpu.CompilerParams(
            collective_id=0, has_side_effects=True, vmem_limit_bytes=56 * 2**20
        ),
        name="schur",
    )(left_panel, upper_inverse, lower_inverse, top_panel, trailing)


def solution(mesh):
    placed = (
        P(("row", "col"), "depth"),
        P(None, "depth"),
        P("depth", None),
        P("depth", "col"),
        P("row", ("col", "depth")),
    )
    return jax.shard_map(
        local, mesh=mesh, in_specs=placed, out_specs=P("row", ("col", "depth")), check_vma=False
    )
```

time: 512 us -> 140 us (0.27)
  waiting for transfers between devices: 458 us -> 0 us
  Pallas kernels: 0 us -> 136 us
  matrix products: 31.3 us -> 0 us
  between operations: 13.1 us -> 0.01 us
    all_gather x3 -> x0, waiting for transfers between devices: 269 us -> none  [the longest x1 166 us: local(): lax.all_gather(top_panel, 'depth', axis=0, tiled=True)]
    reduce_scatter x1 -> x0, waiting for transfers between devices: 188 us -> none  [local(): lax.psum_scatter(lax.dot_general(projected, solved_cols, (((0,), (1,)), (...]
    pallas_call x0 -> x1, Pallas kernels: none -> 136 us  [local(): pl.pallas_call(kernel, out_shape=jax.ShapeDtypeStruct(trailing.shape, F32...]
    dot_general x3 -> x0, matrix products: 31.3 us -> none  [the longest x1 16.7 us: local(): lax.dot_general(projected, solved_cols, (((0,), (1,)), ((), ())), precisi...]
  transfers between devices with their start and end apart: 4 -> 0, of which waited for: 4 -> 0; matrix products, arithmetic and copies ran while one was open for 3% -> 0% of each run, Pallas kernels for 0% -> 0%
where the time goes in v1:
time: 140 us; the launch traced here: 138 us
  Pallas kernels  136 us (97%)
  local copies, waits for them, and re-layouts  2.26 us (2%)
    pallas_call x1, Pallas kernels, local(): pl.pallas_call(kernel, out_shape=jax.ShapeDtypeStruct(trailing.shape, F32...  136 us

profile of v1, /device:TPU:64, one launch (start us, length us, event | category | flops | bytes accessed | tf_op | source)
XLA Modules:
  0.0 137.9 jit_solution(10744181501122829856)
XLA Ops:
  0.0 135.6 %schur.1 = f32[2048,128]{1,0:T(8,128)} custom-call(f32[256,256]{1,0:T(8,128)} %left.1, f32[2048,256]{1,0:T(8,128)} %upper.1, f32[256,2048]{1,0:T(8,128)} %lower.1, f32[256,1024]{1,0:T(8,128)} %top.1, f32[2048,128]{1,0:T(8,128)} %trailing.1), custom_call_target="tpu_custom_call" | custom-call | tf_op jit(solution)/shard_map/schur/pallas_call | solution.py:300
  135.6 2.3 %copy.7 = f32[2048,128]{1,0:T(8,128)} copy(f32[2048,128]{1,0:T(8,128)} %schur.1) | data formatting | bytes 2097152

commit v2 on v1

--- a/solution.py
+++ b/solution.py
@@ -26,8 +26,9 @@
 
 def kernel(
     left, upper, lower, top, trailing, out,
-    gbuf, ubuf, lbuf, sbuf, tloc, tbuf, th, tl, pbuf, rbuf,
-    gsem, xsend, gsend, fsem, fsend, tsem, tsend, rsem, rsend, csem, csend, psem, psend,
+    gbuf, uown, lown, ubuf, lbuf, sbuf, tloc, tbuf, th, tl, pbuf, rbuf, relay,
+    gsem, xsend, gsend, fsem, fsend, tsem, tsend, rsem, rsend, csem, csend,
+    esem, esend, psem, psend, lsem,
 ):
     x = lax.axis_index("row")
     c = lax.axis_index("col")
@@ -43,7 +44,7 @@
         return (x_, lax.rem(z_, 4) * 2 + k_, (z_ // 4) * 4 + y_)
 
     def rot4(v, by):
-        return lax.rem(v + by, 4)
+        return lax.rem(v + by + 4, 4)
 
     def rot8(v, by):
         return lax.rem(v + by + 8, 8)
@@ -58,10 +59,15 @@
 
     zo = rot8(z, 4)
     z_up, z_down = rot8(z, 1), rot8(z, -1)
+    is0, is1 = k == 0, k == 1
+
+    pl.when(is0)(lambda: pltpu.make_async_copy(upper, uown, lsem.at[0]).start())
+    pl.when(is1)(lambda: pltpu.make_async_copy(lower, lown, lsem.at[0]).start())
+    pltpu.make_async_copy(trailing, out, lsem.at[1]).start()
 
     peers = [dev(x, y, z, 1 - k), dev(x, y, zo, 0), dev(x, y, zo, 1), dev(x, y, z_up, k), dev(x, y, z_down, k)]
     peers += [dev(x, rot4(y, i), z, k) for i in (1, 2, 3)]
-    peers += [dev(rot4(x, i), y, z, j) for i in (1, 2, 3) for j in (0, 1)]
+    peers += [dev(rot4(x, i), y, z, j) for i in (1, 3) for j in (0, 1)]
     barrier = pltpu.get_barrier_semaphore()
     for peer in peers:
         pl.semaphore_signal(barrier, inc=1, device_id=peer, device_id_type=MESH)
@@ -98,14 +104,56 @@
     edge = jnp.logical_or(zl == 0, zl == 3)
     z_cross = jnp.where(zl == 0, z_down, z_up)
     z_in = jnp.where(zl == 0, z_up, z_down)
-    uq = upper.at[pl.ds(pl.multiple_of(x * 512, 512), 512), :]
-    lq = lower.at[:, pl.ds(pl.multiple_of(x * 512, 512), 512)]
-    is0, is1 = k == 0, k == 1
-    for is_k, src, buf in ((is0, uq, ubuf), (is1, lq, lbuf)):
-        start(
-            remote(src, buf.at[x], fsend.at[0], fsem.at[x], dev(x, y, z_cross, k)),
-            jnp.logical_and(edge, is_k),
-        )
+
+    def u_share(g, xs, half=None):
+        rows = pl.ds(xs * 128, 128) if half is None else pl.ds(xs * 128 + half * 64, 64)
+        return ubuf.at[g, rows]
+
+    def l_share(g, xs, half=None):
+        rows = pl.ds(xs * 64, 64) if half is None else pl.ds(xs * 64 + half * 32, 32)
+        return lbuf.at[g, rows]
+
+    kinds = ((is0, u_share), (is1, l_share))
+    for g in range(4):
+        uq = upper.at[pl.ds(pl.multiple_of(g * 512 + x * 128, 128), 128), :]
+        lq = lower.at[pl.ds(pl.multiple_of(x * 64, 64), 64), pl.ds(g * 512, 512)]
+        for (is_k, share), src in zip(kinds, (uq, lq)):
+            start(
+                remote(src, share(g, x), fsend.at[g, 0], fsem.at[g, x, 0], dev(x, y, z_cross, k)),
+                jnp.logical_and(jnp.logical_and(edge, is_k), 2 * g <= d),
+            )
+
+    def chunk(g):
+        wanted = 2 * g <= d2
+
+        @pl.when(wanted)
+        def _():
+            landed(u_share(g, x), fsem.at[g, x, 0])
+
+        for is_k, share in kinds:
+            go = jnp.logical_and(wanted, is_k)
+            r = share(g, x)
+            start(
+                remote(r, r, fsend.at[g, 1], fsem.at[g, x, 0], dev(x, y, z_in, k)), jnp.logical_and(edge, go)
+            )
+            start(remote(r, r, fsend.at[g, 2], fsem.at[g, x, 0], dev(rot4(x, 1), y, z, k)), go)
+            start(remote(r, r, fsend.at[g, 3], fsem.at[g, x, 0], dev(rot4(x, -1), y, z, k)), go)
+
+    def chunk_relay(g):
+        wanted = 2 * g <= d2
+        for half, by in ((0, 1), (1, -1)):
+            xs = rot4(x, -by)
+
+            @pl.when(wanted)
+            def _():
+                landed(u_share(g, xs), fsem.at[g, xs, 0])
+
+            for is_k, share in kinds:
+                r = share(g, xs, half)
+                start(
+                    remote(r, r, fsend.at[g, 4 + half], fsem.at[g, xs, half], dev(rot4(x, by), y, z, k)),
+                    jnp.logical_and(wanted, is_k),
+                )
 
     def gather_y(slot, j):
         for i in (1, 2, 3):
@@ -117,32 +165,32 @@
 
     landed(gbuf.at[d], gsem.at[d])
     gather_y(d, 0)
-    landed(ubuf.at[0], fsem.at[x])
-    for is_k, buf in ((is0, ubuf), (is1, lbuf)):
-        start(
-            remote(buf.at[x], buf.at[x], fsend.at[1], fsem.at[x], dev(x, y, z_in, k)),
-            jnp.logical_and(edge, is_k),
-        )
-        for i in (1, 2, 3):
-            start(
-                remote(buf.at[x], buf.at[x], fsend.at[1 + i], fsem.at[x], dev(rot4(x, i), y, z, k)),
-                is_k,
-            )
+    chunk(0)
     landed(gbuf.at[d2], gsem.at[d2])
     gather_y(d2, 1)
+    chunk(1)
+    chunk_relay(0)
+    chunk(2)
+    chunk_relay(1)
+    chunk(3)
+    chunk_relay(2)
+    chunk_relay(3)
+
+    landed(uown, lsem.at[0])
 
     def wait_block(i):
-        other_y = lax.rem(i, 4) != y
-
-        @pl.when(jnp.logical_and(other_y, i <= 4 + y))
+        @pl.when(jnp.logical_and(lax.rem(i, 4) != y, i <= 4 + y))
         def _():
             landed(gbuf.at[i], gsem.at[i])
 
-        q = i // 2
-
-        @pl.when(jnp.logical_and(lax.rem(i, 2) == 0, q != x))
+    def wait_chunk(i):
+        g = i // 2
+        xs = rot4(x, 2)
+
+        @pl.when(jnp.logical_and(lax.rem(i, 2) == 0, i <= d2))
         def _():
-            landed(ubuf.at[q], fsem.at[q])
+            landed(u_share(g, xs, 0), fsem.at[g, xs, 0])
+            landed(u_share(g, xs, 1), fsem.at[g, xs, 1])
 
     @pl.when(k == 0)
     def _():
@@ -151,10 +199,11 @@
         @pl.loop(0, 8)
         def _(i):
             wait_block(i)
+            wait_chunk(i)
 
             @pl.when(i <= d)
             def _():
-                f = upper[pl.ds(pl.multiple_of(i * B, B), B), :]
+                f = uown[pl.ds(pl.multiple_of(i * B, B), B), :]
                 sbuf[z, zh] += mm3(split(gbuf[i]), split(f))
 
             @pl.when(i <= d2)
@@ -174,10 +223,11 @@
         @pl.loop(0, 8)
         def _(i):
             wait_block(i)
+            wait_chunk(i)
 
             @pl.when(i <= d)
             def _():
-                f = lower[:, pl.ds(pl.multiple_of(i * B, B), B)]
+                f = lown[:, pl.ds(pl.multiple_of(i * B, B), B)]
                 tloc[zh] += mm3(split(f), split(gbuf[i]))
 
             @pl.when(i <= d2)
@@ -185,15 +235,19 @@
                 f = lbuf[i // 2, :, pl.ds(pl.multiple_of(lax.rem(i, 2) * B, B), B)]
                 tloc[1 - zh] += mm3(split(f), split(gbuf[i]))
 
-    for i in range(4):
+    for i, by in enumerate((0, 1, -1)):
         own = jnp.logical_and(t_core == 1, i == 0)
-        start(
-            remote(tloc, tbuf.at[t_slot], tsend.at[i], tsem.at[t_slot], dev(rot4(x, i), y, z, t_core)),
-            jnp.logical_and(is1, jnp.logical_not(own)),
+        for n in (0, 1):
+            start(
+                remote(
+                    tloc.at[n], tbuf.at[t_slot, n], tsend.at[i, n], tsem.at[t_slot, n], dev(rot4(x, by), y, z, t_core)
+                ),
+                jnp.logical_and(is1, jnp.logical_not(own)),
+            )
+    for n in (0, 1):
+        pl.when(jnp.logical_and(is1, t_core == 1))(
+            lambda: pltpu.make_async_copy(tloc.at[n], tbuf.at[t_slot, n], tsem.at[t_slot, n]).start()
         )
-    pl.when(jnp.logical_and(is1, t_core == 1))(
-        lambda: pltpu.make_async_copy(tloc, tbuf.at[t_slot], tsem.at[t_slot]).start()
-    )
 
     def piece(i):
         s = (i + 1) // 2
@@ -221,10 +275,17 @@
     def rows_of(p):
         return pl.ds(pl.multiple_of((2 * lax.rem(p, 4) + p // 4) * B, B), B)
 
-    def partial_copy(i, j):
-        rows = rows_of(piece(i))
-        yy = rot4(y, j)
-        return remote(pbuf.at[i, yy], rbuf.at[j - 1, rows], psend.at[j - 1, i], psem.at[j - 1, i], dev(x, yy, z, k))
+    ups = ((0, 1), (1, -1))
+
+    def relay_copy(i, n, by):
+        r = pbuf.at[i, rot4(y, 2), pl.ds(n * 128, 128)]
+        return remote(r, relay.at[n, i], esend.at[n, i], esem.at[n, i], dev(x, rot4(y, by), z, k))
+
+    def partial_copy(i, n, by):
+        yy = rot4(y, by)
+        return remote(
+            pbuf.at[i, yy], rbuf.at[n, rows_of(piece(i))], psend.at[n, i], psem.at[n, i], dev(x, yy, z, k)
+        )
 
     def process(i):
         p = piece(i)
@@ -234,9 +295,17 @@
             acc = mm3(a[0], (th[h, 0], tl[h, 0])) + mm3(a[1], (th[h, 1], tl[h, 1]))
             pbuf[i, 2 * h] = acc[:, :128]
             pbuf[i, 2 * h + 1] = acc[:, 128:]
-        for j in (1, 2, 3):
-            partial_copy(i, j).start()
-        out[rows, :] = trailing[rows, :] - pbuf[i, y]
+        for n, by in ups:
+            relay_copy(i, n, by).start()
+        out[rows, :] = out[rows, :] - pbuf[i, y]
+
+    def pass_on(i):
+        for n, by in ups:
+            landed(relay.at[n, i], esem.at[n, i])
+            yy = rot4(y, by)
+            part = pl.ds(n * 128, 128)
+            pbuf[i, yy, part] = pbuf[i, yy, part] + relay[n, i]
+            partial_copy(i, n, by).start()
 
     @pl.when(k == 1)
     def _():
@@ -245,30 +314,40 @@
     ring(z, rsend.at[0], 1, z_up).start()
     ring(z, rsend.at[8], 2, z_down).start()
 
+    def t_relay(xs, n, by):
+        r = tbuf.at[lax.rem(xs, 2), n]
+        return remote(r, r, tsend.at[3, 0], tsem.at[lax.rem(xs, 2), n], dev(rot4(x, by), y, z, k))
+
     for h in (0, 1):
-        landed(tbuf.at[h], tsem.at[h])
+        xs = 2 * k + h
+        for n, by in ups:
+            landed(tbuf.at[h, n], tsem.at[h, n])
+            start(t_relay(xs, n, by), xs == rot4(x, -by))
         for n in (0, 1):
             high, low = split(tbuf[h, n])
             th[h, n] = high
             tl[h, n] = low
 
+    landed(out, lsem.at[1])
     process(0)
 
-    @pl.loop(1, 9)
+    @pl.loop(1, 10)
     def _(i):
         pl.when(i < 8)(lambda: arrive(i))
 
-        @pl.when(i > 1)
+        @pl.when(jnp.logical_and(i > 1, i < 9))
         def _():
             landed(sbuf.at[piece(i - 1), :, other_half, :], csem.at[i - 1])
             process(i - 1)
 
+        pl.when(i > 1)(lambda: pass_on(i - 2))
+
     @pl.loop(0, 8)
     def _(i):
         rows = rows_of(piece(i))
-        for j in (1, 2, 3):
-            landed(rbuf.at[j - 1, rows], psem.at[j - 1, i])
-        out[rows, :] = out[rows, :] - ((rbuf[0, rows] + rbuf[1, rows]) + rbuf[2, rows])
+        for n in (0, 1):
+            landed(rbuf.at[n, rows], psem.at[n, i])
+        out[rows, :] = out[rows, :] - (rbuf[0, rows] + rbuf[1, rows])
 
     for cp, when in sends:
         if when is None:
@@ -290,8 +369,9 @@
 
     @pl.loop(0, 8)
     def _(i):
-        for j in (1, 2, 3):
-            partial_copy(i, j).wait_send()
+        for n, by in ups:
+            relay_copy(i, n, by).wait_send()
+            partial_copy(i, n, by).wait_send()
 
 
 def local(left_panel, upper_inverse, lower_inverse, top_panel, trailing):
@@ -300,10 +380,12 @@
     return pl.pallas_call(
         kernel,
         out_shape=jax.ShapeDtypeStruct(trailing.shape, F32),
-        in_specs=[vmem] * 5,
+        in_specs=[pl.BlockSpec(memory_space=pl.ANY)] * 5,
         out_specs=vmem,
         scratch_shapes=[
             pltpu.VMEM((8, B, B), F32),
+            pltpu.VMEM((2048, B), F32),
+            pltpu.VMEM((B, 2048), F32),
             pltpu.VMEM((4, 512, B), F32),
             pltpu.VMEM((4, B, 512), F32),
             pltpu.VMEM((8, 2, B, B), F32),
@@ -312,12 +394,14 @@
             pltpu.VMEM((2, 2, B, B), BF16),
             pltpu.VMEM((2, 2, B, B), BF16),
             pltpu.VMEM((8, 4, B, 128), F32),
-            pltpu.VMEM((3, 2048, 128), F32),
-            dma((8,)), dma((3,)), dma((2, 3)), dma((4,)), dma((5,)), dma((2,)), dma((4,)),
-            dma((8,)), dma((9,)), dma((8,)), dma((8,)), dma((3, 8)), dma((3, 8)),
+            pltpu.VMEM((2, 2048, 128), F32),
+            pltpu.VMEM((2, 8, 128, 128), F32),
+            dma((8,)), dma((3,)), dma((2, 3)), dma((4, 4, 2)), dma((4, 6)), dma((2, 2)), dma((4, 2)),
+            dma((8,)), dma((9,)), dma((8,)), dma((8,)),
+            dma((2, 8)), dma((2, 8)), dma((2, 8)), dma((2, 8)), dma((2,)),
         ],
         compiler_params=pltpu.CompilerParams(
-            collective_id=0, has_side_effects=True, vmem_limit_bytes=56 * 2**20
+            collective_id=0, has_side_effects=True, vmem_limit_bytes=60 * 2**20
         ),
         name="schur",
     )(left_panel, upper_inverse, lower_inverse, top_panel, trailing)

time: 140 us -> 107 us (0.76)
  the two profiles are of different devices: /device:TPU:64 before, /device:TPU:38 now
where the time goes in v2:
time: 107 us
  Pallas kernels  105 us (98%)
  local copies, waits for them, and re-layouts  2.26 us (2%)
    pallas_call x1, Pallas kernels, local(): pl.pallas_call(kernel, out_shape=jax.ShapeDtypeStruct(trailing.shape, F32...  105 us
    unnamed x1, local copies, waits for them, and re-layouts  2.26 us

profile of v2, /device:TPU:38, one launch (start us, length us, event | category | flops | bytes accessed | tf_op | source)
XLA Modules:
  0.0 107.2 jit_solution(3289711066658226556)
XLA Ops:
  0.0 105.0 %schur.1 = f32[2048,128]{1,0:T(8,128)} custom-call(f32[256,256]{1,0:T(8,128)} %left.1, f32[2048,256]{1,0:T(8,128)} %upper.1, f32[256,2048]{1,0:T(8,128)} %lower.1, f32[256,1024]{1,0:T(8,128)} %top.1, f32[2048,128]{1,0:T(8,128)} %trailing.1), custom_call_target="tpu_custom_call" | custom-call | tf_op jit(solution)/shard_map/schur/pallas_call | solution.py:380
  105.0 2.3 %copy.7 = f32[2048,128]{1,0:T(8,128)} copy(f32[2048,128]{1,0:T(8,128)} %schur.1) | data formatting | bytes 2097152

commit v3 on v2

--- a/solution.py
+++ b/solution.py
@@ -25,10 +25,10 @@
 
 
 def kernel(
-    left, upper, lower, top, trailing, out,
-    gbuf, uown, lown, ubuf, lbuf, sbuf, tloc, tbuf, th, tl, pbuf, rbuf, relay,
+    left, upper, lower, top, trailing, result,
+    out, gbuf, uown, lown, ubuf, lbuf, sbuf, tloc, tbuf, th, tl, pbuf, rbuf, relay,
     gsem, xsend, gsend, fsem, fsend, tsem, tsend, rsem, rsend, csem, csend,
-    esem, esend, psem, psend, lsem,
+    esem, esend, psem, psend, lsem, osem, go,
 ):
     x = lax.axis_index("row")
     c = lax.axis_index("col")
@@ -83,10 +83,10 @@
         sends.append((cp, when))
 
     is_self = jnp.logical_and(k == 0, zh == 0)
-    start(
-        remote(left, gbuf.at[d], xsend.at[0], gsem.at[d], dev(x, y, k * 4 + zl, 0)),
-        jnp.logical_not(is_self),
-    )
+    def send_left(when):
+        start(remote(left, gbuf.at[d], xsend.at[0], gsem.at[d], dev(x, y, k * 4 + zl, 0)), when)
+
+    send_left(jnp.logical_and(k == zh, jnp.logical_not(is_self)))
     pl.when(is_self)(lambda: pltpu.make_async_copy(left, gbuf.at[d], gsem.at[d]).start())
 
     mine = k == x // 2
@@ -114,14 +114,14 @@
         return lbuf.at[g, rows]
 
     kinds = ((is0, u_share), (is1, l_share))
-    for g in range(4):
+    def feed(g, kind):
         uq = upper.at[pl.ds(pl.multiple_of(g * 512 + x * 128, 128), 128), :]
         lq = lower.at[pl.ds(pl.multiple_of(x * 64, 64), 64), pl.ds(g * 512, 512)]
-        for (is_k, share), src in zip(kinds, (uq, lq)):
-            start(
-                remote(src, share(g, x), fsend.at[g, 0], fsem.at[g, x, 0], dev(x, y, z_cross, k)),
-                jnp.logical_and(jnp.logical_and(edge, is_k), 2 * g <= d),
-            )
+        is_k, share = kinds[kind]
+        start(
+            remote((uq, lq)[kind], share(g, x), fsend.at[g, 0], fsem.at[g, x, 0], dev(x, y, z_cross, k)),
+            jnp.logical_and(jnp.logical_and(edge, is_k), 2 * g <= d),
+        )
 
     def chunk(g):
         wanted = 2 * g <= d2
@@ -163,12 +163,26 @@
                 jnp.logical_or(slot < 4, yy > y),
             )
 
+    feed(0, 1)
+    feed(1, 1)
+    feed(2, 1)
+    feed(3, 1)
     landed(gbuf.at[d], gsem.at[d])
     gather_y(d, 0)
+    pl.when(is0)(lambda: pl.semaphore_wait(go, 1))
+    send_left(jnp.logical_and(is0, zh == 1))
+    feed(0, 0)
+    feed(1, 0)
+    feed(2, 0)
+    feed(3, 0)
     chunk(0)
+    pl.when(is1)(
+        lambda: pl.semaphore_signal(go, inc=1, device_id=dev(x, y, z, 0), device_id_type=MESH)
+    )
+    send_left(jnp.logical_and(is1, zh == 0))
+    chunk(1)
     landed(gbuf.at[d2], gsem.at[d2])
     gather_y(d2, 1)
-    chunk(1)
     chunk_relay(0)
     chunk(2)
     chunk_relay(1)
@@ -314,16 +328,16 @@
     ring(z, rsend.at[0], 1, z_up).start()
     ring(z, rsend.at[8], 2, z_down).start()
 
-    def t_relay(xs, n, by):
-        r = tbuf.at[lax.rem(xs, 2), n]
-        return remote(r, r, tsend.at[3, 0], tsem.at[lax.rem(xs, 2), n], dev(rot4(x, by), y, z, k))
-
+    rel = rot4(x, -2 * k)
+    t_near = 1 - lax.rem(rel, 2)
+    t_half = jnp.where(jnp.logical_or(rel == 0, rel == 3), 1, 0)
+    r = tbuf.at[t_near, t_half]
+    landed(r, tsem.at[t_near, t_half])
+    start(remote(r, r, tsend.at[3, 0], tsem.at[t_near, t_half], dev(rot4(x, 1 - 2 * t_half), y, z, k)))
     for h in (0, 1):
-        xs = 2 * k + h
-        for n, by in ups:
-            landed(tbuf.at[h, n], tsem.at[h, n])
-            start(t_relay(xs, n, by), xs == rot4(x, -by))
         for n in (0, 1):
+            here = jnp.logical_and(t_near == h, t_half == n)
+            pl.when(jnp.logical_not(here))(lambda: landed(tbuf.at[h, n], tsem.at[h, n]))
             high, low = split(tbuf[h, n])
             th[h, n] = high
             tl[h, n] = low
@@ -348,6 +362,7 @@
         for n in (0, 1):
             landed(rbuf.at[n, rows], psem.at[n, i])
         out[rows, :] = out[rows, :] - (rbuf[0, rows] + rbuf[1, rows])
+        pltpu.make_async_copy(out.at[rows], result.at[rows], osem.at[i]).start()
 
     for cp, when in sends:
         if when is None:
@@ -372,17 +387,19 @@
         for n, by in ups:
             relay_copy(i, n, by).wait_send()
             partial_copy(i, n, by).wait_send()
+        rows = rows_of(piece(i))
+        pltpu.make_async_copy(out.at[rows], result.at[rows], osem.at[i]).wait()
 
 
 def local(left_panel, upper_inverse, lower_inverse, top_panel, trailing):
-    vmem = pl.BlockSpec(memory_space=pltpu.VMEM)
     dma = pltpu.SemaphoreType.DMA
     return pl.pallas_call(
         kernel,
         out_shape=jax.ShapeDtypeStruct(trailing.shape, F32),
         in_specs=[pl.BlockSpec(memory_space=pl.ANY)] * 5,
-        out_specs=vmem,
+        out_specs=pl.BlockSpec(memory_space=pl.ANY),
         scratch_shapes=[
+            pltpu.VMEM((2048, 128), F32),
             pltpu.VMEM((8, B, B), F32),
             pltpu.VMEM((2048, B), F32),
             pltpu.VMEM((B, 2048), F32),
@@ -398,7 +415,7 @@
             pltpu.VMEM((2, 8, 128, 128), F32),
             dma((8,)), dma((3,)), dma((2, 3)), dma((4, 4, 2)), dma((4, 6)), dma((2, 2)), dma((4, 2)),
             dma((8,)), dma((9,)), dma((8,)), dma((8,)),
-            dma((2, 8)), dma((2, 8)), dma((2, 8)), dma((2, 8)), dma((2,)),
+            dma((2, 8)), dma((2, 8)), dma((2, 8)), dma((2, 8)), dma((2,)), dma((8,)), pltpu.SemaphoreType.REGULAR,
         ],
         compiler_params=pltpu.CompilerParams(
             collective_id=0, has_side_effects=True, vmem_limit_bytes=60 * 2**20

time: 107 us -> 101 us (0.944)
  the two profiles are of different devices: /device:TPU:38 before, /device:TPU:64 now
where the time goes in v3:
time: 101 us; the launch traced here: 98.7 us
  Pallas kernels  96.4 us (95%)
  local copies, waits for them, and re-layouts  2.26 us (2%)
    pallas_call x1, Pallas kernels, local(): pl.pallas_call(kernel, out_shape=jax.ShapeDtypeStruct(trailing.shape, F32...  96.4 us
    unnamed x1, local copies, waits for them, and re-layouts  2.26 us

profile of v3, /device:TPU:64, one launch (start us, length us, event | category | flops | bytes accessed | tf_op | source)
XLA Modules:
  0.0 98.7 jit_solution(10153911728479090492)
XLA Ops:
  0.0 96.4 %schur.1 = f32[2048,128]{1,0:T(8,128)} custom-call(f32[256,256]{1,0:T(8,128)} %left.1, f32[2048,256]{1,0:T(8,128)} %upper.1, f32[256,2048]{1,0:T(8,128)} %lower.1, f32[256,1024]{1,0:T(8,128)} %top.1, f32[2048,128]{1,0:T(8,128)} %trailing.1), custom_call_target="tpu_custom_call" | custom-call | tf_op jit(solution)/shard_map/schur/pallas_call | solution.py:396
  96.4 2.3 %copy.7 = f32[2048,128]{1,0:T(8,128)} copy(f32[2048,128]{1,0:T(8,128)} %schur.1) | data formatting | bytes 2097152

commit v4 on v3

--- a/solution.py
+++ b/solution.py
@@ -213,19 +213,22 @@
         @pl.loop(0, 8)
         def _(i):
             wait_block(i)
-            wait_chunk(i)
 
             @pl.when(i <= d)
             def _():
                 f = uown[pl.ds(pl.multiple_of(i * B, B), B), :]
                 sbuf[z, zh] += mm3(split(gbuf[i]), split(f))
 
+        @pl.loop(0, 8)
+        def _(i):
+            wait_chunk(i)
+
             @pl.when(i <= d2)
             def _():
                 f = ubuf[i // 2, pl.ds(pl.multiple_of(lax.rem(i, 2) * B, B), B), :]
                 sbuf[z, 1 - zh] += mm3(split(gbuf[i]), split(f))
 
-        remote(sbuf.at[z], sbuf.at[z], csend.at[0], csem.at[0], dev(x, y, z, 1)).start()
+        remote(sbuf.at[z], sbuf.at[z], csend.at[0, 0], csem.at[0, 0], dev(x, y, z, 1)).start()
 
     t_core = x // 2
     t_slot = lax.rem(x, 2)
@@ -237,12 +240,15 @@
         @pl.loop(0, 8)
         def _(i):
             wait_block(i)
-            wait_chunk(i)
 
             @pl.when(i <= d)
             def _():
                 f = lown[:, pl.ds(pl.multiple_of(i * B, B), B)]
                 tloc[zh] += mm3(split(f), split(gbuf[i]))
+
+        @pl.loop(0, 8)
+        def _(i):
+            wait_chunk(i)
 
             @pl.when(i <= d2)
             def _():
@@ -267,24 +273,33 @@
         s = (i + 1) // 2
         return rot8(z, jnp.where(lax.rem(i, 2) == 1, -s, s))
 
-    half = pl.ds(pl.multiple_of(k * 128, 128), 128)
-    other_half = pl.ds(pl.multiple_of((1 - k) * 128, 128), 128)
-
-    def ring(p, ss, i, z_):
-        r = sbuf.at[p, :, half, :]
-        return remote(r, r, ss, rsem.at[i], dev(x, y, z_, k))
-
-    def to_sibling(p, i):
-        r = sbuf.at[p, :, half, :]
-        return remote(r, r, csend.at[i], csem.at[i], dev(x, y, z, 1 - k))
+    def quarter(p, core, q):
+        return sbuf.at[p, :, pl.ds(pl.multiple_of(core * 128 + q * 64, 64), 64), :]
+
+    def ring(p, ss, i, q, z_):
+        r = quarter(p, k, q)
+        return remote(r, r, ss, rsem.at[i, q], dev(x, y, z_, k))
+
+    def to_sibling(p, i, q):
+        r = quarter(p, k, q)
+        return remote(r, r, csend.at[i, q], csem.at[i, q], dev(x, y, z, 1 - k))
+
+    def ring_on(p, i, q):
+        odd = lax.rem(i, 2) == 1
+        go = jnp.where(odd, i < 7 - 2 * q, i < 5 + 2 * q)
+        return ring(p, rsend.at[i, q], jnp.minimum(i + 2, 7), q, jnp.where(odd, z_up, z_down)), go
 
     def arrive(i):
         p = piece(i)
-        landed(sbuf.at[p, :, half, :], rsem.at[i])
-        odd = lax.rem(i, 2) == 1
-        pl.when(jnp.logical_and(odd, i < 7))(lambda: ring(p, rsend.at[i], i + 2, z_up).start())
-        pl.when(jnp.logical_and(jnp.logical_not(odd), i < 6))(lambda: ring(p, rsend.at[i], i + 2, z_down).start())
-        to_sibling(p, i).start()
+        for q in (0, 1):
+            landed(quarter(p, k, q), rsem.at[i, q])
+            cp, go = ring_on(p, i, q)
+            pl.when(go)(lambda: cp.start())
+            to_sibling(p, i, q).start()
+
+    def whole(i):
+        for q in (0, 1):
+            landed(quarter(piece(i), 1 - k, q), csem.at[i, q])
 
     def rows_of(p):
         return pl.ds(pl.multiple_of((2 * lax.rem(p, 4) + p // 4) * B, B), B)
@@ -295,10 +310,12 @@
         r = pbuf.at[i, rot4(y, 2), pl.ds(n * 128, 128)]
         return remote(r, relay.at[n, i], esend.at[n, i], esem.at[n, i], dev(x, rot4(y, by), z, k))
 
-    def partial_copy(i, n, by):
+    def partial_copy(i, n, by, m):
         yy = rot4(y, by)
+        rows = pl.ds(pl.multiple_of(rows_of(piece(i)).start + m * 128, 128), 128)
         return remote(
-            pbuf.at[i, yy], rbuf.at[n, rows_of(piece(i))], psend.at[n, i], psem.at[n, i], dev(x, yy, z, k)
+            pbuf.at[i, yy, pl.ds(m * 128, 128)], rbuf.at[n, rows], psend.at[n, m, i], psem.at[n, m, i],
+            dev(x, yy, z, k),
         )
 
     def process(i):
@@ -311,6 +328,7 @@
             pbuf[i, 2 * h + 1] = acc[:, 128:]
         for n, by in ups:
             relay_copy(i, n, by).start()
+            partial_copy(i, n, by, 1 - n).start()
         out[rows, :] = out[rows, :] - pbuf[i, y]
 
     def pass_on(i):
@@ -319,14 +337,15 @@
             yy = rot4(y, by)
             part = pl.ds(n * 128, 128)
             pbuf[i, yy, part] = pbuf[i, yy, part] + relay[n, i]
-            partial_copy(i, n, by).start()
+            partial_copy(i, n, by, n).start()
 
     @pl.when(k == 1)
     def _():
-        landed(sbuf.at[z], csem.at[0])
-
-    ring(z, rsend.at[0], 1, z_up).start()
-    ring(z, rsend.at[8], 2, z_down).start()
+        landed(sbuf.at[z], csem.at[0, 0])
+
+    for q in (0, 1):
+        ring(z, rsend.at[0, q], 1, q, z_up).start()
+        ring(z, rsend.at[8, q], 2, q, z_down).start()
 
     rel = rot4(x, -2 * k)
     t_near = 1 - lax.rem(rel, 2)
@@ -345,22 +364,24 @@
     landed(out, lsem.at[1])
     process(0)
 
-    @pl.loop(1, 10)
+    arrive(1)
+
+    @pl.loop(1, 9)
     def _(i):
-        pl.when(i < 8)(lambda: arrive(i))
-
-        @pl.when(jnp.logical_and(i > 1, i < 9))
+        @pl.when(i < 8)
         def _():
-            landed(sbuf.at[piece(i - 1), :, other_half, :], csem.at[i - 1])
-            process(i - 1)
-
-        pl.when(i > 1)(lambda: pass_on(i - 2))
+            whole(i)
+            process(i)
+
+        pl.when(i < 7)(lambda: arrive(i + 1))
+        pass_on(i - 1)
 
     @pl.loop(0, 8)
     def _(i):
         rows = rows_of(piece(i))
         for n in (0, 1):
-            landed(rbuf.at[n, rows], psem.at[n, i])
+            for m in (0, 1):
+                landed(rbuf.at[n, pl.ds(pl.multiple_of(rows.start + m * 128, 128), 128)], psem.at[n, m, i])
         out[rows, :] = out[rows, :] - (rbuf[0, rows] + rbuf[1, rows])
         pltpu.make_async_copy(out.at[rows], result.at[rows], osem.at[i]).start()
 
@@ -372,21 +393,25 @@
 
     @pl.when(k == 0)
     def _():
-        remote(sbuf.at[z], sbuf.at[z], csend.at[0], csem.at[0], dev(x, y, z, 1)).wait_send()
-
-    ring(z, rsend.at[0], 1, z_up).wait_send()
-    ring(z, rsend.at[8], 2, z_down).wait_send()
+        remote(sbuf.at[z], sbuf.at[z], csend.at[0, 0], csem.at[0, 0], dev(x, y, z, 1)).wait_send()
+
+    for q in (0, 1):
+        ring(z, rsend.at[0, q], 1, q, z_up).wait_send()
+        ring(z, rsend.at[8, q], 2, q, z_down).wait_send()
 
     @pl.loop(1, 8)
     def _(i):
-        pl.when(i < 6)(lambda: ring(z, rsend.at[i], i + 2, z_up).wait_send())
-        to_sibling(z, i).wait_send()
+        for q in (0, 1):
+            cp, go = ring_on(z, i, q)
+            pl.when(go)(lambda: cp.wait_send())
+            to_sibling(z, i, q).wait_send()
 
     @pl.loop(0, 8)
     def _(i):
         for n, by in ups:
             relay_copy(i, n, by).wait_send()
-            partial_copy(i, n, by).wait_send()
+            for m in (0, 1):
+                partial_copy(i, n, by, m).wait_send()
         rows = rows_of(piece(i))
         pltpu.make_async_copy(out.at[rows], result.at[rows], osem.at[i]).wait()
 
@@ -414,8 +439,8 @@
             pltpu.VMEM((2, 2048, 128), F32),
             pltpu.VMEM((2, 8, 128, 128), F32),
             dma((8,)), dma((3,)), dma((2, 3)), dma((4, 4, 2)), dma((4, 6)), dma((2, 2)), dma((4, 2)),
-            dma((8,)), dma((9,)), dma((8,)), dma((8,)),
-            dma((2, 8)), dma((2, 8)), dma((2, 8)), dma((2, 8)), dma((2,)), dma((8,)), pltpu.SemaphoreType.REGULAR,
+            dma((8, 2)), dma((9, 2)), dma((8, 2)), dma((8, 2)),
+            dma((2, 8)), dma((2, 8)), dma((2, 2, 8)), dma((2, 2, 8)), dma((2,)), dma((8,)), pltpu.SemaphoreType.REGULAR,
         ],
         compiler_params=pltpu.CompilerParams(
             collective_id=0, has_side_effects=True, vmem_limit_bytes=60 * 2**20

time: 101 us -> 99.2 us (0.982); the launches traced: 98.7 us -> 98.7 us
  no operation moved by 1% of the time
where the time goes in v4:
time: 99.2 us; the launch traced here: 98.7 us
  Pallas kernels  96.4 us (97%)
  local copies, waits for them, and re-layouts  2.26 us (2%)
    pallas_call x1, Pallas kernels, local(): pl.pallas_call(kernel, out_shape=jax.ShapeDtypeStruct(trailing.shape, F32...  96.4 us
    unnamed x1, local copies, waits for them, and re-layouts  2.26 us

profile of v4, /device:TPU:64, one launch (start us, length us, event | category | flops | bytes accessed | tf_op | source)
XLA Modules:
  0.0 98.7 jit_solution(527174376437243757)
XLA Ops:
  0.0 96.4 %schur.1 = f32[2048,128]{1,0:T(8,128)} custom-call(f32[256,256]{1,0:T(8,128)} %left.1, f32[2048,256]{1,0:T(8,128)} %upper.1, f32[256,2048]{1,0:T(8,128)} %lower.1, f32[256,1024]{1,0:T(8,128)} %top.1, f32[2048,128]{1,0:T(8,128)} %trailing.1), custom_call_target="tpu_custom_call" | custom-call | tf_op jit(solution)/shard_map/schur/pallas_call | solution.py:421
  96.4 2.3 %copy.7 = f32[2048,128]{1,0:T(8,128)} copy(f32[2048,128]{1,0:T(8,128)} %schur.1) | data formatting | bytes 2097152

commit v5 on v4

--- a/solution.py
+++ b/solution.py
@@ -181,10 +181,10 @@
     )
     send_left(jnp.logical_and(is1, zh == 0))
     chunk(1)
+    chunk_relay(0)
+    chunk(2)
     landed(gbuf.at[d2], gsem.at[d2])
     gather_y(d2, 1)
-    chunk_relay(0)
-    chunk(2)
     chunk_relay(1)
     chunk(3)
     chunk_relay(2)
@@ -269,6 +269,14 @@
             lambda: pltpu.make_async_copy(tloc.at[n], tbuf.at[t_slot, n], tsem.at[t_slot, n]).start()
         )
 
+    rel = rot4(x, -2 * k)
+    t_near = 1 - lax.rem(rel, 2)
+    t_half = jnp.where(jnp.logical_or(rel == 0, rel == 3), 1, 0)
+    r = tbuf.at[t_near, t_half]
+    pass_t = remote(r, r, tsend.at[3, 0], tsem.at[t_near, t_half], dev(rot4(x, 1 - 2 * t_half), y, z, k))
+    pl.when(is1)(lambda: landed(r, tsem.at[t_near, t_half]))
+    start(pass_t, is1)
+
     def piece(i):
         s = (i + 1) // 2
         return rot8(z, jnp.where(lax.rem(i, 2) == 1, -s, s))
@@ -319,15 +327,17 @@
         )
 
     def process(i):
+        rows = rows_of(piece(i))
         p = piece(i)
-        rows = rows_of(p)
-        a = [split(sbuf[p, n]) for n in (0, 1)]
-        for h in (0, 1):
-            acc = mm3(a[0], (th[h, 0], tl[h, 0])) + mm3(a[1], (th[h, 1], tl[h, 1]))
+        a = split(jnp.concatenate([sbuf[p, 0], sbuf[p, 1]], axis=1))
+        for n_h, h in enumerate((1 - y // 2, y // 2)):
+            acc = mm3(a, (th[h].reshape(2 * B, B), tl[h].reshape(2 * B, B)))
             pbuf[i, 2 * h] = acc[:, :128]
             pbuf[i, 2 * h + 1] = acc[:, 128:]
+            if n_h == 0:
+                for n, by in ups:
+                    relay_copy(i, n, by).start()
         for n, by in ups:
-            relay_copy(i, n, by).start()
             partial_copy(i, n, by, 1 - n).start()
         out[rows, :] = out[rows, :] - pbuf[i, y]
 
@@ -347,12 +357,8 @@
         ring(z, rsend.at[0, q], 1, q, z_up).start()
         ring(z, rsend.at[8, q], 2, q, z_down).start()
 
-    rel = rot4(x, -2 * k)
-    t_near = 1 - lax.rem(rel, 2)
-    t_half = jnp.where(jnp.logical_or(rel == 0, rel == 3), 1, 0)
-    r = tbuf.at[t_near, t_half]
-    landed(r, tsem.at[t_near, t_half])
-    start(remote(r, r, tsend.at[3, 0], tsem.at[t_near, t_half], dev(rot4(x, 1 - 2 * t_half), y, z, k)))
+    pl.when(is0)(lambda: landed(r, tsem.at[t_near, t_half]))
+    start(pass_t, is0)
     for h in (0, 1):
         for n in (0, 1):
             here = jnp.logical_and(t_near == h, t_half == n)
@@ -373,8 +379,8 @@
             whole(i)
             process(i)
 
+        pass_on(i - 1)
         pl.when(i < 7)(lambda: arrive(i + 1))
-        pass_on(i - 1)
 
     @pl.loop(0, 8)
     def _(i):

time: 99.2 us -> 98.8 us (level)
  no operation moved by 1% of the time
where the time goes in v5:
time: 98.8 us; the launch traced here: 98.7 us
  Pallas kernels  96.4 us (98%)
  local copies, waits for them, and re-layouts  2.26 us (2%)
    pallas_call x1, Pallas kernels, local(): pl.pallas_call(kernel, out_shape=jax.ShapeDtypeStruct(trailing.shape, F32...  96.4 us
    unnamed x1, local copies, waits for them, and re-layouts  2.26 us

profile of v5, /device:TPU:64, one launch (start us, length us, event | category | flops | bytes accessed | tf_op | source)
XLA Modules:
  0.0 98.7 jit_solution(13267342806079881690)
XLA Ops:
  0.0 96.4 %schur.1 = f32[2048,128]{1,0:T(8,128)} custom-call(f32[256,256]{1,0:T(8,128)} %left.1, f32[2048,256]{1,0:T(8,128)} %upper.1, f32[256,2048]{1,0:T(8,128)} %lower.1, f32[256,1024]{1,0:T(8,128)} %top.1, f32[2048,128]{1,0:T(8,128)} %trailing.1), custom_call_target="tpu_custom_call" | custom-call | tf_op jit(solution)/shard_map/schur/pallas_call | solution.py:427
  96.4 2.3 %copy.7 = f32[2048,128]{1,0:T(8,128)} copy(f32[2048,128]{1,0:T(8,128)} %schur.1) | data formatting | bytes 2097152

commit v6 on v5

--- a/solution.py
+++ b/solution.py
@@ -65,6 +65,13 @@
     pl.when(is1)(lambda: pltpu.make_async_copy(lower, lown, lsem.at[0]).start())
     pltpu.make_async_copy(trailing, out, lsem.at[1]).start()
 
+    is_self = jnp.logical_and(k == 0, zh == 0)
+    pl.when(is_self)(lambda: pltpu.make_async_copy(left, gbuf.at[d], gsem.at[d]).start())
+    kept = top.at[:, pl.ds(pl.multiple_of(zh * 512 + lax.rem(x, 2) * B, B), B)]
+    pl.when(jnp.logical_and(is1, x // 2 == 1))(
+        lambda: pltpu.make_async_copy(kept, gbuf.at[d], gsem.at[d]).start()
+    )
+
     peers = [dev(x, y, z, 1 - k), dev(x, y, zo, 0), dev(x, y, zo, 1), dev(x, y, z_up, k), dev(x, y, z_down, k)]
     peers += [dev(x, rot4(y, i), z, k) for i in (1, 2, 3)]
     peers += [dev(rot4(x, i), y, z, j) for i in (1, 3) for j in (0, 1)]
@@ -82,12 +89,10 @@
             pl.when(when)(lambda: cp.start())
         sends.append((cp, when))
 
-    is_self = jnp.logical_and(k == 0, zh == 0)
     def send_left(when):
         start(remote(left, gbuf.at[d], xsend.at[0], gsem.at[d], dev(x, y, k * 4 + zl, 0)), when)
 
     send_left(jnp.logical_and(k == zh, jnp.logical_not(is_self)))
-    pl.when(is_self)(lambda: pltpu.make_async_copy(left, gbuf.at[d], gsem.at[d]).start())
 
     mine = k == x // 2
     for h in (0, 1):
@@ -96,9 +101,6 @@
         start(
             remote(block, gbuf.at[d], xsend.at[1 + h], gsem.at[d], dev(x, y, h * 4 + zl, 1)),
             jnp.logical_and(mine, jnp.logical_not(own)),
-        )
-        pl.when(jnp.logical_and(mine, own))(
-            lambda: pltpu.make_async_copy(block, gbuf.at[d], gsem.at[d]).start()
         )
 
     edge = jnp.logical_or(zl == 0, zl == 3)

time: 98.8 us -> 98.8 us (level)
  no operation moved by 1% of the time
where the time goes in v6:
time: 98.8 us; the launch traced here: 98.7 us
  Pallas kernels  96.4 us (98%)
  local copies, waits for them, and re-layouts  2.26 us (2%)
    pallas_call x1, Pallas kernels, local(): pl.pallas_call(kernel, out_shape=jax.ShapeDtypeStruct(trailing.shape, F32...  96.4 us
    unnamed x1, local copies, waits for them, and re-layouts  2.26 us

profile of v6, /device:TPU:64, one launch (start us, length us, event | category | flops | bytes accessed | tf_op | source)
XLA Modules:
  0.0 98.7 jit_solution(3948873269509820899)
XLA Ops:
  0.0 96.4 %schur.1 = f32[2048,128]{1,0:T(8,128)} custom-call(f32[256,256]{1,0:T(8,128)} %left.1, f32[2048,256]{1,0:T(8,128)} %upper.1, f32[256,2048]{1,0:T(8,128)} %lower.1, f32[256,1024]{1,0:T(8,128)} %top.1, f32[2048,128]{1,0:T(8,128)} %trailing.1), custom_call_target="tpu_custom_call" | custom-call | tf_op jit(solution)/shard_map/schur/pallas_call | solution.py:429
  96.4 2.3 %copy.7 = f32[2048,128]{1,0:T(8,128)} copy(f32[2048,128]{1,0:T(8,128)} %schur.1) | data formatting | bytes 2097152
